TPU v7x, 256 devices: a whole 4x4x8 slice. The times are simulated.
256 devices in a mesh: outer: 16 (over z_lo, y, core), inner: 16 (over z_hi, x).
Axes of the slice: x: 4, y: 4, z: 8 (z_hi: 4, z_lo: 2; z = z_hi * 2 + z_lo), core: 2. Of those that a mesh axis runs over, the one named last changes fastest.
Arguments:
- queries: bfloat16 [8192, 2048], P(('outer', 'inner')), may hold values from -9 to 9
- keys: bfloat16 [8192, 2048], P(('outer', 'inner')), may hold values from -9 to 9
- values: bfloat16 [8192, 2048], P(('outer', 'inner')), may hold values from -6 to 6
- outputs: bfloat16 [8192, 2048], P(('outer', 'inner')), may hold values from -2 to 2
- out_grads: bfloat16 [8192, 2048], P(('outer', 'inner')), may hold values from -6 to 6
Outputs:
- query_grads: bfloat16 [8192, 2048], P(('outer', 'inner'))
- key_grads: bfloat16 [8192, 2048], P(('outer', 'inner'))
- value_grads: bfloat16 [8192, 2048], P(('outer', 'inner'))
All inputs are finite; a program needn't handle non-finite values.
Results may differ from a plain program's by a relative error of at most 0.0049.
Values may be sent and summed in bfloat16 or wider, within the bound.
A program may use at most 64 MiB of HBM per device.

v0:
```python
import math

import jax
import jax.numpy as jnp
from jax import lax
from jax.sharding import PartitionSpec as P

HEAD_DIM = 128


def score_block(query_rows, key_rows, softmax_scale):
    return (
        jnp.einsum("qhd,khd->hqk", query_rows, key_rows, preferred_element_type=jnp.float32)
        * softmax_scale
    )


def online_update(running, scores):
    top_score, total_mass = running
    top_new = jnp.maximum(top_score, jnp.max(scores, axis=2))
    mass_new = total_mass * jnp.exp(top_score - top_new) + jnp.sum(
        jnp.exp(scores - top_new[..., None]), axis=2
    )
    return (top_new, mass_new)


def body(queries, keys, values, outputs, out_grads):
    tok_rows = queries.shape[0]
    heads_all = queries.shape[1] // HEAD_DIM
    softmax_scale = HEAD_DIM ** (-0.5)

    def split_heads(array):
        return array.reshape(tok_rows, heads_all, HEAD_DIM)

    queries_here, keys_here, values_here, outs_here, grads_here = (
        lax.all_to_all(split_heads(queries), "inner", split_axis=1, concat_axis=0, tiled=True),
        lax.all_to_all(split_heads(keys), "inner", split_axis=1, concat_axis=0, tiled=True),
        lax.all_to_all(split_heads(values), "inner", split_axis=1, concat_axis=0, tiled=True),
        lax.all_to_all(split_heads(outputs), "inner", split_axis=1, concat_axis=0, tiled=True),
        lax.all_to_all(split_heads(out_grads), "inner", split_axis=1, concat_axis=0, tiled=True),
    )
    node_rows = queries_here.shape[0]
    head_loc = queries_here.shape[1]
    all_rows = node_rows * lax.axis_size("outer")
    block_rows = math.gcd(512, all_rows)
    count_blocks = all_rows // block_rows
    row_delta = jnp.sum(grads_here.astype(jnp.float32) * outs_here.astype(jnp.float32), axis=2).T
    start_stats = (
        jnp.full((head_loc, node_rows), -jnp.inf, jnp.float32),
        jnp.zeros((head_loc, node_rows), jnp.float32),
    )
    zero_rows = jnp.zeros((node_rows, head_loc, HEAD_DIM), jnp.float32)
    keys_all, values_all = (
        lax.all_gather(keys_here, "outer", axis=0, tiled=True),
        lax.all_gather(values_here, "outer", axis=0, tiled=True),
    )
    key_blocks = keys_all.reshape(count_blocks, block_rows, head_loc, HEAD_DIM)
    value_blocks = values_all.reshape(count_blocks, block_rows, head_loc, HEAD_DIM)

    def stat_step(running, key_block):
        return (online_update(running, score_block(queries_here, key_block, softmax_scale)), None)

    (top_score, total_mass), unused = lax.scan(stat_step, start_stats, key_blocks)
    log_norm = top_score + jnp.log(total_mass)

    def grad_step(query_acc, pair):
        key_block, value_block = pair
        probs = jnp.exp(score_block(queries_here, key_block, softmax_scale) - log_norm[..., None])
        prob_half = probs.astype(jnp.bfloat16)
        value_part = jnp.einsum(
            "hqk,qhd->khd", prob_half, grads_here, preferred_element_type=jnp.float32
        )
        prob_grad = jnp.einsum(
            "qhd,khd->hqk", grads_here, value_block, preferred_element_type=jnp.float32
        )
        score_half = (probs * (prob_grad - row_delta[..., None]) * softmax_scale).astype(
            jnp.bfloat16
        )
        query_acc = query_acc + jnp.einsum(
            "hqk,khd->qhd", score_half, key_block, preferred_element_type=jnp.float32
        )
        key_part = jnp.einsum(
            "hqk,qhd->khd", score_half, queries_here, preferred_element_type=jnp.float32
        )
        return (query_acc, (key_part, value_part))

    query_acc, (key_parts, value_parts) = lax.scan(grad_step, zero_rows, (key_blocks, value_blocks))
    key_acc, value_acc = (
        lax.psum_scatter(
            key_parts.reshape(all_rows, head_loc, HEAD_DIM),
            "outer",
            scatter_dimension=0,
            tiled=True,
        ),
        lax.psum_scatter(
            value_parts.reshape(all_rows, head_loc, HEAD_DIM),
            "outer",
            scatter_dimension=0,
            tiled=True,
        ),
    )
    query_back, key_back, value_back = (
        lax.all_to_all(
            query_acc.astype(jnp.bfloat16), "inner", split_axis=0, concat_axis=1, tiled=True
        ),
        lax.all_to_all(
            key_acc.astype(jnp.bfloat16), "inner", split_axis=0, concat_axis=1, tiled=True
        ),
        lax.all_to_all(
            value_acc.astype(jnp.bfloat16), "inner", split_axis=0, concat_axis=1, tiled=True
        ),
    )
    flat_width = heads_all * HEAD_DIM
    return (
        query_back.reshape(tok_rows, flat_width),
        key_back.reshape(tok_rows, flat_width),
        value_back.reshape(tok_rows, flat_width),
    )


def solution(mesh):
    return jax.shard_map(
        body,
        mesh=mesh,
        in_specs=(
            P(("outer", "inner"), None),
            P(("outer", "inner"), None),
            P(("outer", "inner"), None),
            P(("outer", "inner"), None),
            P(("outer", "inner"), None),
        ),
        out_specs=(
            P(("outer", "inner"), None),
            P(("outer", "inner"), None),
            P(("outer", "inner"), None),
        ),
        check_vma=False,
    )
```

profile of v0, /device:TPU:1, one launch (start us, length us, event | category | flops | bytes accessed | tf_op | source)
XLA Modules:
  0.0 378.8 jit_solution(12172837916527255958)
XLA Ops:
  8.1 20.7 %all_to_all.126 = bf16[32,16,128]{2,0,1:T(8,128)(2,1)} all-to-all(bf16[32,16,128]{2,0,1:T(8,128)(2,1)S(1)} %copy_bitcast_fusion.7), channel_id=1, replica_groups=mesh['outer'=16,'inner'=16] {'inner'}, dimensions={1} | all-to-all | bytes 262144 | tf_op jit(solution)/shard_map/all_to_all | solution.py:37
  28.9 1.6 copy_bitcast_fusion.4
  30.4 3.5 all-to-all-start.3
  34.0 1.6 copy_bitcast_fusion.3
  35.5 7.7 %all-to-all-done.3 = bf16[32,16,128]{2,0,1:T(8,128)(2,1)S(1)} async-done(((bf16[32,16,128]{2,0,1:T(8,128)(2,1)}), bf16[32,16,128]{2,0,1:T(8,128)(2,1)S(1)}, u32[]{:S(2)}, u32[]{:S(2)}) %all-to-all-start.3) | async-done | bytes 131104 | tf_op jit(solution)/shard_map/all_to_all | solution.py:40
  43.2 3.5 all-to-all-start.4
  46.8 1.6 copy_bitcast_fusion.5
  48.4 7.8 %all-to-all-done.4 = bf16[32,16,128]{2,0,1:T(8,128)(2,1)S(1)} async-done(((bf16[32,16,128]{2,0,1:T(8,128)(2,1)}), bf16[32,16,128]{2,0,1:T(8,128)(2,1)S(1)}, u32[]{:S(2)}, u32[]{:S(2)}) %all-to-all-start.4) | async-done | bytes 131104 | tf_op jit(solution)/shard_map/all_to_all | solution.py:39
  56.2 3.5 all-to-all-start.2
  59.7 1.6 copy_bitcast_fusion.6
  61.3 7.5 %all-to-all-done.2 = bf16[32,16,128]{2,0,1:T(8,128)(2,1)S(1)} async-done(((bf16[32,16,128]{2,0,1:T(8,128)(2,1)}), bf16[32,16,128]{2,0,1:T(8,128)(2,1)S(1)}, u32[]{:S(2)}, u32[]{:S(2)}) %all-to-all-start.2) | async-done | bytes 131104 | tf_op jit(solution)/shard_map/all_to_all | solution.py:38
  68.8 3.5 all-to-all-start.1
  73.1 8.4 %all-to-all-done.1 = bf16[32,16,128]{2,0,1:T(8,128)(2,1)S(1)} async-done(((bf16[32,16,128]{2,0,1:T(8,128)(2,1)}), bf16[32,16,128]{2,0,1:T(8,128)(2,1)S(1)}, u32[]{:S(2)}, u32[]{:S(2)}) %all-to-all-start.1) | async-done | bytes 131104 | tf_op jit(solution)/shard_map/all_to_all | solution.py:36
  81.5 23.7 %while.28 = (s32[]{:T(128)}, f32[1,512]{1,0:T(1,128)S(1)}, f32[1,512]{1,0:T(1,128)S(1)}, bf16[16,512,1,128]{3,1,2,0:T(8,128)(2,1)}, bf16[512,1,128]{2,0,1:T(8,128)(2,1)S(1)}, /*index=5*/s32[]{:T(128)}, s32[]{:T(128)}) while((s32[]{:T(128)}, f32[1,512]{1,0:T(1,128)S(1)}, f32[1,512]{1,0:T(1,128)S(1)}, ...), condition=%wide.region_3.0_spmd.clone, body=%wide.region_0.3_spmd.clone.sunk | while | flops 68160000 | bytes 2386520 | solution.py:63
  81.5 1.2 fusion.57
  83.0 1.2 fusion.57
  84.4 1.2 fusion.57
  85.9 1.2 fusion.57
  87.4 1.2 fusion.57
  88.9 1.2 fusion.57
  90.3 1.2 fusion.57
  91.8 1.2 fusion.57
  93.3 1.2 fusion.57
  94.8 1.3 fusion.57
  96.3 1.2 fusion.57
  97.8 1.2 fusion.57
  99.3 1.2 fusion.57
  100.7 1.2 fusion.57
  102.2 1.2 fusion.57
  103.7 1.2 fusion.57
  105.2 15.3 %all-gather.5.cloned.1.call-done = bf16[8192,1,128]{2,0,1:T(8,128)(2,1)} async-done(((bf16[512,1,128]{2,0,1:T(8,128)(2,1)}), bf16[8192,1,128]{2,0,1:T(8,128)(2,1)}) %all-gather.5.cloned.1.call-update) | async-done | bytes 2097168 | tf_op jit(solution)/shard_map/all_gather | solution.py:55
  120.5 90.1 %while.29 = (s32[]{:T(128)}, f32[512,1,128]{0,2,1:T(8,128)S(1)}, f32[16,512,1,128]{3,1,2,0:T(8,128)}, f32[16,512,1,128]{3,1,2,0:T(8,128)}, bf16[16,512,1,128]{3,...) while((s32[]{:T(128)}, f32[512,1,128]{0,2,1:T(8,128)S(1)}, ...), condition=%wide.region_6.7_spmd.clone, body=%wide.region_5.6_spmd.clone.sunk | while | flops 337510400 | bytes 6691455 | solution.py:87
  120.5 1.2 fusion.70
  121.8 1.2 fusion.71
  126.1 1.2 fusion.70
  127.4 1.2 fusion.71
  131.8 1.2 fusion.70
  133.0 1.2 fusion.71
  137.4 1.2 fusion.70
  138.7 1.2 fusion.71
  143.1 1.2 fusion.70
  144.3 1.2 fusion.71
  148.7 1.2 fusion.70
  149.9 1.2 fusion.71
  154.4 1.2 fusion.70
  160.0 1.2 fusion.70
  165.6 1.2 fusion.70
  171.2 1.2 fusion.70
  176.8 1.2 fusion.70
  182.4 1.2 fusion.70
  188.1 1.2 fusion.70
  193.7 1.2 fusion.70
  194.9 1.2 fusion.71
  199.4 1.2 fusion.70
  205.0 1.2 fusion.70
  206.2 1.2 fusion.71
  213.3 8.8 %all-to-all-start.5 = ((bf16[16,2,2048]{2,1,0:T(2,128)(2,1)}), bf16[16,2,2048]{2,1,0:T(2,128)(2,1)S(1)}, u32[]{:S(2)}, u32[]{:S(2)}) async-start(bf16[16,2,2048]{2,1,0:T(2,128)(2,1)} %reshape.135), calls=%async_computation.5 | async-start | bytes 262144 | tf_op jit(solution)/shard_map/all_to_all | solution.py:103
  222.1 55.8 %reduce-scatter.3.cloned.1.call-done = f32[512,1,128]{2,1,0:T(1,128)} async-done(((f32[8192,1,128]{2,1,0:T(1,128)}), f32[512,1,128]{2,1,0:T(1,128)}) %reduce-scatter.3.cloned.1.call-update) | async-done | bytes 262160 | tf_op jit(solution)/shard_map/reduce_scatter | solution.py:89
  279.1 1.4 reduce.10
  281.2 10.0 %all-to-all-start.6 = ((bf16[16,2,2048]{2,1,0:T(2,128)(2,1)}), bf16[16,2,2048]{2,1,0:T(2,128)(2,1)S(1)}, u32[]{:S(2)}, u32[]{:S(2)}) async-start(bf16[16,2,2048]{2,1,0:T(2,128)(2,1)} %reshape.137), calls=%async_computation.7 | async-start | bytes 262144 | tf_op jit(solution)/shard_map/all_to_all | solution.py:106
  291.2 58.5 %reduce-scatter.5.cloned.1.call-done = f32[512,1,128]{2,1,0:T(1,128)} async-done(((f32[8192,1,128]{2,1,0:T(1,128)}), f32[512,1,128]{2,1,0:T(1,128)}) %reduce-scatter.5.cloned.1.call-update) | async-done | bytes 262160 | tf_op jit(solution)/shard_map/reduce_scatter | solution.py:95
  350.8 1.4 reduce.9
  352.9 9.1 %all-to-all-start.7 = ((bf16[16,2,2048]{2,1,0:T(2,128)(2,1)}), bf16[16,2,2048]{2,1,0:T(2,128)(2,1)S(1)}, u32[]{:S(2)}, u32[]{:S(2)}) async-start(bf16[16,2,2048]{2,1,0:T(2,128)(2,1)} %reshape.139), calls=%async_computation.9 | async-start | bytes 262144 | tf_op jit(solution)/shard_map/all_to_all | solution.py:109
  363.2 8.1 %all-to-all-done.7 = bf16[16,2,2048]{2,1,0:T(2,128)(2,1)S(1)} async-done(((bf16[16,2,2048]{2,1,0:T(2,128)(2,1)}), bf16[16,2,2048]{2,1,0:T(2,128)(2,1)S(1)}, u32[]{:S(2)}, u32[]{:S(2)}) %all-to-all-start.7) | async-done | bytes 131104 | tf_op jit(solution)/shard_map/all_to_all | solution.py:109
  (164 shorter events, 74.3 us)
Async XLA Ops:
  7.2 0.9 copy-start
  7.2 74.3 %all-gather.3.cloned.1.call-start = ((), (), s32[]{:S(2)}) async-start(), calls=%async_computation.10 | async-start | bytes 2228224 | tf_op jit(solution)/shard_map/all_gather | solution.py:54
  30.4 12.8 %all-to-all-start.3 = ((bf16[32,16,128]{2,0,1:T(8,128)(2,1)}), bf16[32,16,128]{2,0,1:T(8,128)(2,1)S(1)}, u32[]{:S(2)}, u32[]{:S(2)}) async-start(bf16[32,16,128]{2,0,1:T(8,128)(2,1)} %copy_bitcast_fusion.4), calls=%async_computation.3 | async-start | bytes 262144 | tf_op jit(solution)/shard_map/all_to_all | solution.py:40
  43.2 13.0 %all-to-all-start.4 = ((bf16[32,16,128]{2,0,1:T(8,128)(2,1)}), bf16[32,16,128]{2,0,1:T(8,128)(2,1)S(1)}, u32[]{:S(2)}, u32[]{:S(2)}) async-start(bf16[32,16,128]{2,0,1:T(8,128)(2,1)} %copy_bitcast_fusion.3), calls=%async_computation.4 | async-start | bytes 262144 | tf_op jit(solution)/shard_map/all_to_all | solution.py:39
  56.2 12.6 %all-to-all-start.2 = ((bf16[32,16,128]{2,0,1:T(8,128)(2,1)}), bf16[32,16,128]{2,0,1:T(8,128)(2,1)S(1)}, u32[]{:S(2)}, u32[]{:S(2)}) async-start(bf16[32,16,128]{2,0,1:T(8,128)(2,1)} %copy_bitcast_fusion.5), calls=%async_computation.2 | async-start | bytes 262144 | tf_op jit(solution)/shard_map/all_to_all | solution.py:38
  68.8 3.9 %copy-start.1 = (bf16[32,16,128]{2,0,1:T(8,128)(2,1)}, bf16[32,16,128]{2,0,1:T(8,128)(2,1)S(1)}, u32[]{:S(2)}) copy-start(bf16[32,16,128]{2,0,1:T(8,128)(2,1)S(1)} %all-to-all-done.2) | copy-start | bytes 393220
  68.8 12.7 %all-to-all-start.1 = ((bf16[32,16,128]{2,0,1:T(8,128)(2,1)}), bf16[32,16,128]{2,0,1:T(8,128)(2,1)S(1)}, u32[]{:S(2)}, u32[]{:S(2)}) async-start(bf16[32,16,128]{2,0,1:T(8,128)(2,1)} %copy_bitcast_fusion.6), calls=%async_computation.1 | async-start | bytes 262144 | tf_op jit(solution)/shard_map/all_to_all | solution.py:36
  72.3 48.2 %all-gather.5.cloned.1.call-start = ((), (), s32[]{:S(2)}) async-start(), calls=%async_computation.11 | async-start | bytes 2228224 | tf_op jit(solution)/shard_map/all_gather | solution.py:55
  73.1 204.9 %reduce-scatter.3.cloned.1.call-start = ((), (), s32[]{:S(2)}) async-start(), calls=%async_computation.12 | async-start | bytes 4456448 | tf_op jit(solution)/shard_map/reduce_scatter | solution.py:89
  210.7 139.0 %reduce-scatter.5.cloned.1.call-start = ((), (), s32[]{:S(2)}) async-start(), calls=%async_computation.13 | async-start | bytes 4456448 | tf_op jit(solution)/shard_map/reduce_scatter | solution.py:95
  213.3 67.9 %all-to-all-start.5 = ((bf16[16,2,2048]{2,1,0:T(2,128)(2,1)}), bf16[16,2,2048]{2,1,0:T(2,128)(2,1)S(1)}, u32[]{:S(2)}, u32[]{:S(2)}) async-start(bf16[16,2,2048]{2,1,0:T(2,128)(2,1)} %reshape.135), calls=%async_computation.5 | async-start | bytes 262144 | tf_op jit(solution)/shard_map/all_to_all | solution.py:103
  281.2 71.8 %all-to-all-start.6 = ((bf16[16,2,2048]{2,1,0:T(2,128)(2,1)}), bf16[16,2,2048]{2,1,0:T(2,128)(2,1)S(1)}, u32[]{:S(2)}, u32[]{:S(2)}) async-start(bf16[16,2,2048]{2,1,0:T(2,128)(2,1)} %reshape.137), calls=%async_computation.7 | async-start | bytes 262144 | tf_op jit(solution)/shard_map/all_to_all | solution.py:106
  352.9 18.4 %all-to-all-start.7 = ((bf16[16,2,2048]{2,1,0:T(2,128)(2,1)}), bf16[16,2,2048]{2,1,0:T(2,128)(2,1)S(1)}, u32[]{:S(2)}, u32[]{:S(2)}) async-start(bf16[16,2,2048]{2,1,0:T(2,128)(2,1)} %reshape.139), calls=%async_computation.9 | async-start | bytes 262144 | tf_op jit(solution)/shard_map/all_to_all | solution.py:109
Sparse Core Ops, SparseCore 0:
  29.0 34.6 all-gather.2
  75.6 44.9 all-gather.4
  210.8 67.1 reduce-scatter.2
  280.3 69.3 reduce-scatter.4
where the time goes:
time: 383 us; the launch traced here: 379 us
  waiting for transfers between devices  170 us (44%)
  matrix products  109 us (28%)
  starting transfers between devices  42.2 us (11%)
  blocking collectives  20.7 us (5%)
  between operations  14 us (4%)
  local copies, waits for them, and re-layouts  12.1 us (3%)
  other arithmetic  9.47 us (2%)
    reduce_scatter x1, waiting for transfers between devices, body(): lax.psum_scatter(value_parts.reshape(all_rows, head_loc, HEAD_DIM), 'oute...  58.5 us
    reduce_scatter x1, waiting for transfers between devices, body(): lax.psum_scatter(key_parts.reshape(all_rows, head_loc, HEAD_DIM), 'outer'...  55.8 us
    dot_general x32, matrix products, score_block(): jnp.einsum('qhd,khd->hqk', query_rows, key_rows, preferred_element_type=j...  38.9 us
    all_to_all x1, blocking collectives, body(): lax.all_to_all(split_heads(keys), 'inner', split_axis=1, concat_axis=0, t...  20.7 us
    dot_general x16, matrix products, grad_step(): jnp.einsum('qhd,khd->hqk', grads_here, value_block, preferred_element_typ...  19.3 us
    dot_general x16, matrix products, grad_step(): jnp.einsum('hqk,khd->qhd', score_half, key_block, preferred_element_type=...  18.8 us
    dot_general x16, matrix products, grad_step(): jnp.einsum('hqk,qhd->khd', prob_half, grads_here, preferred_element_type=...  16.3 us
    dot_general x16, matrix products, grad_step(): jnp.einsum('hqk,qhd->khd', score_half, queries_here, preferred_element_ty...  16 us
  transfers between devices with their start and end apart: 11, of which 8 were waited for; matrix products, arithmetic and copies ran while one was open for 10% of the time, Pallas kernels for 0%

commit v1 on v0

v1 whole, which is shorter than its diff:
```python
import functools

import jax
import jax.numpy as jnp
import numpy as np
from jax import lax
from jax.experimental import pallas as pl
from jax.experimental.pallas import tpu as pltpu
from jax.sharding import PartitionSpec as P

HEAD_DIM = 128
MESH = pl.DeviceIdType.MESH
NT = (((1,), (1,)), ((), ()))
NN = (((1,), (0,)), ((), ()))
LOG2E = float(np.log2(np.e))
S1_ORDER = (0, 2, 1, 3)
VMEM_LIMIT = 62 << 20
VG_AT = 3


def dot(a, b, dims):
    return lax.dot_general(a, b, dims, preferred_element_type=jnp.float32)


def kernel(
    cfg,
    q_in, k_in, v_in, o_in, g_in,
    dq_out, dk_out, dv_out,
    qg, kg, vg, gg, kt, e_s, m_s, l_s, f_s,
    own_o, own_g, d_stage, d_slot, d_all, st, st_in, dqt, dk_s, dv_s, sib_buf, sib_in, z_buf, z_in, dqb, dq_in, fin,
    in_sem, s1_send, s1_recv, s1_loc, d_send, d_recv,
    kv_send, kv_recv, qg_send, qg_recv, st_send, st_recv,
    sib_send, sib_recv, z_send, z_recv, dq_send, dq_recv, out_send, out_recv, out_loc,
):
    H, NX, NY, T, TK = cfg
    NZ = 2 * (H // NX)
    D = HEAD_DIM
    B = H * T
    G = B // 4
    per = H // 4
    scale = D ** (-0.5)
    c_log = scale * LOG2E
    halves = B // TK

    o = lax.axis_index("outer")
    i = lax.axis_index("inner")
    c = lax.rem(o, 2)
    y = lax.rem(lax.div(o, 2), NY)
    zl = lax.div(o, 2 * NY)
    x = lax.rem(i, NX)
    z = 2 * lax.div(i, NX) + zl
    up = 2 * zl - 1

    def dev(z_, y_, c_, x_):
        return ((lax.rem(z_, 2) * NY + y_) * 2 + c_, lax.div(z_, 2) * NX + x_)

    def along(dz, dx):
        return dev(lax.rem(z + dz + NZ, NZ), y, c, lax.rem(x + dx, NX))

    def there(r):
        g, dx = r // NX, r % NX
        return along((0, -2 * up, up, 3 * up)[g], dx)

    def back(r):
        g, dx = r // NX, r % NX
        return along((0, 2 * up, up, 3 * up)[g], NX - dx)

    sib = dev(z, y, 1 - c, x)
    zpart = dev(z - up, y, c, x)
    diag = dev(z - up, y, 1 - c, x)

    def ring(t):
        return dev(z, lax.rem(y + t, NY), c, x)

    def remote(src, dst, ssem, rsem, device):
        pltpu.make_async_remote_copy(
            src_ref=src, dst_ref=dst, send_sem=ssem, recv_sem=rsem, device_id=device, device_id_type=MESH
        ).start()

    def wait_for(ref, sem):
        pltpu.make_async_copy(ref, ref, sem).wait()

    def cols(h):
        return pl.ds(pl.multiple_of(h * D, D), D)

    cp_g = pltpu.make_async_copy(g_in, own_g, in_sem.at[0])
    cp_o = pltpu.make_async_copy(o_in, own_o, in_sem.at[1])
    cp_g.start()
    cp_o.start()

    barrier = pltpu.get_barrier_semaphore()
    partners = [there(r) for r in range(H - 1, 0, -1)] + [back(NX + dx) for dx in range(NX)]
    partners += [ring(2), ring(1), ring(3), diag, zpart, sib]
    for p in partners:
        pl.semaphore_signal(barrier, inc=1, device_id=p, device_id_type=MESH)

    pl.semaphore_wait(barrier, len(partners))

    PLACE = (3, 1, 2, 0)

    def part(s, g):
        return pl.ds(g * B + PLACE[s] * G, G)

    def group(g):
        return pl.ds(g * B, B)

    s1 = ((k_in, kg), (q_in, qg), (v_in, vg), (g_in, gg))

    def s1_sends(pair):
        for a in pair:
            src, dst = s1[a]
            pltpu.make_async_copy(src.at[:, cols(i)], dst.at[pl.ds(PLACE[0] * G, T), :], s1_loc.at[a]).start()
        for g in S1_ORDER:
            for j in range(per):
                r = g * per + j
                if r == 0:
                    continue
                to = there(r)
                for a in pair:
                    src, dst = s1[a]
                    remote(
                        src.at[:, cols(to[1])],
                        dst.at[pl.ds(g * B + PLACE[0] * G + j * T, T), :],
                        s1_send.at[a],
                        s1_recv.at[a, g],
                        to,
                    )

    s1_sends((0, 1))
    if VG_AT == 0:
        s1_sends((2, 3))

    cp_g.wait()
    cp_o.wait()
    prod = own_g[...].astype(jnp.float32) * own_o[...].astype(jnp.float32)
    prod4 = jnp.concatenate([prod] * 4, axis=0)
    pick = (
        lax.broadcasted_iota(jnp.int32, (H, H * D), 0) == lax.broadcasted_iota(jnp.int32, (H, H * D), 1) // D
    ).astype(jnp.float32)
    delta = lax.dot_general(
        pick, prod4, NT, precision=lax.Precision.HIGHEST, preferred_element_type=jnp.float32
    )
    for h in range(H):
        d_stage[h] = delta[h : h + 1, :]
    d_slot[0] = d_stage[i]
    for r in range(1, H):
        to = there(r)
        remote(d_stage.at[to[1]], d_slot.at[r], d_send, d_recv, to)

    def arrived(a, g):
        dst = s1[a][1]
        if g == 0:
            wait_for(dst.at[pl.ds(PLACE[0] * G, T), :], s1_loc.at[a])
            if G > T:
                wait_for(dst.at[pl.ds(PLACE[0] * G + T, G - T), :], s1_recv.at[a, g])
        else:
            wait_for(dst.at[part(0, g), :], s1_recv.at[a, g])

    def first(n, g):
        kv, qd = (kg, vg)[n], (qg, gg)[n]
        arrived(2 * n, g)
        remote(kv.at[part(0, g), :], kv.at[part(2, g), :], kv_send.at[n, 2, g], kv_recv.at[n, 2, g], zpart)
        remote(kv.at[part(0, g), :], kv.at[part(1, g), :], kv_send.at[n, 1, g], kv_recv.at[n, 1, g], sib)
        arrived(2 * n + 1, g)
        for t in (2, 1, 3):
            remote(qd.at[part(0, g), :], qd.at[part(t, g), :], qg_send.at[n, t - 1, g], qg_recv.at[n, t - 1, g], ring(t))

    def forward(n, g):
        kv = (kg, vg)[n]
        wait_for(kv.at[part(2, g), :], kv_recv.at[n, 2, g])
        remote(kv.at[part(2, g), :], kv.at[part(3, g), :], kv_send.at[n, 0, g], kv_recv.at[n, 0, g], sib)

    def complete(n, g):
        kv, qd = (kg, vg)[n], (qg, gg)[n]
        for t in (1, 3, 2):
            wait_for(qd.at[part(t, g), :], qg_recv.at[n, t - 1, g])
        wait_for(kv.at[part(1, g), :], kv_recv.at[n, 1, g])
        wait_for(kv.at[part(3, g), :], kv_recv.at[n, 0, g])

    def stats(*blocks):
        for gq, gk in blocks:
            for h in range(halves):
                kc = gk * halves + h
                ks = pl.ds(kc * TK, TK)
                s = dot(kg[ks, :], qg[group(gq), :], NT)
                m = jnp.max(s, axis=0, keepdims=True) * c_log
                e = jnp.exp2(s * c_log - m)
                e_s[ks, group(gq)] = e
                m_s[pl.ds(kc, 1), group(gq)] = m
                l_s[pl.ds(kc, 1), group(gq)] = jnp.sum(e, axis=0, keepdims=True)

    lane = lax.broadcasted_iota(jnp.int32, (1, 128), 1) // T

    def stats_send(g):
        m = m_s[:, group(g)]
        top = jnp.max(m, axis=0, keepdims=True)
        total = jnp.sum(l_s[:, group(g)] * jnp.exp2(m - top), axis=0, keepdims=True)
        st[g, :, pl.ds(0, B)] = top + jnp.log2(total)
        st[g, :, pl.ds(B, 128)] = sum(jnp.where(lane == j, d_slot[per * g + j], 0.0) for j in range(per))
        for t in (2, 1, 3):
            remote(st.at[g], st_in.at[t - 1, g], st_send.at[t - 1, g], st_recv.at[t - 1, g], ring(t))

    def lanes(s):
        return pl.ds(PLACE[s] * G, G)

    def stats_take(g):
        for t in (1, 3, 2):
            wait_for(st_in.at[t - 1, g], st_recv.at[t - 1, g])
        for s in range(4):
            parts = [st[g, :, lanes(s)]] + [st_in[t - 1, g, :, lanes((s - t) % 4)] for t in (1, 2, 3)]
            top = functools.reduce(jnp.maximum, parts)
            norm = top + jnp.log2(sum(jnp.exp2(p - top) for p in parts))
            f_s[:, part(s, g)] = jnp.exp2(m_s[:, part(s, g)] - norm)
            delta_rows = st[g, :, pl.ds(B, G)] if s == 0 else st_in[s - 1, g, :, pl.ds(B, G)]
            d_all[pl.ds(0, 1), part(s, g)] = delta_rows

    def transpose_keys(g):
        kt[:, group(g)] = kg[group(g), :].T

    a, b, c3, d = S1_ORDER
    for n, g in enumerate(S1_ORDER):
        first(0, g)
        if n:
            forward(0, S1_ORDER[n - 1])
        if VG_AT == n + 1:
            s1_sends((2, 3))
    complete(0, a)
    stats((a, a))
    forward(0, d)
    complete(0, b)
    stats((a, b), (b, a), (b, b))
    complete(0, c3)
    stats((a, c3), (b, c3), (c3, a), (c3, b), (c3, c3))
    first(1, a)
    complete(0, d)
    wait_for(d_slot.at[pl.ds(1, H - 1)], d_recv)
    stats((a, d), (b, d), (c3, d))
    for g in (a, b, c3):
        stats_send(g)
    first(1, b)
    stats((d, a), (d, b), (d, c3), (d, d))
    stats_send(d)
    first(1, c3)
    forward(1, a)
    first(1, d)
    for g in (b, c3, d):
        forward(1, g)
    for g in range(4):
        transpose_keys(g)
    for g in range(4):
        complete(1, g)

    seen = set()

    def block(gq, gk):
        start_q, start_k = (gq, "q") not in seen, (gk, "k") not in seen
        seen.update(((gq, "q"), (gk, "k")))
        gv = gg[group(gq), :]
        qv = qg[group(gq), :]
        dp = dot(vg[group(gk), :], gv, NT)
        p = jnp.concatenate(
            [
                e_s[pl.ds(gk * B + h * TK, TK), group(gq)] * f_s[pl.ds(gk * halves + h, 1), group(gq)]
                for h in range(halves)
            ],
            axis=0,
        )
        ds = (p * ((dp - d_all[pl.ds(0, 1), group(gq)]) * scale)).astype(jnp.bfloat16)
        dv = dot(p.astype(jnp.bfloat16), gv, NN)
        dk = dot(ds, qv, NN)
        dq = dot(kt[:, group(gk)], ds, NN)
        dv_s[group(gk), :] = dv if start_k else dv_s[group(gk), :] + dv
        dk_s[group(gk), :] = dk if start_k else dk_s[group(gk), :] + dk
        dqt[:, group(gq)] = dq if start_q else dqt[:, group(gq)] + dq

    outs = (dq_out, dk_out, dv_out)

    def send_back(a, g):
        for j in range(per):
            r = g * per + j
            here = fin.at[a, pl.ds(r * T, T), :]
            if r == 0:
                pltpu.make_async_copy(here, outs[a].at[:, cols(i)], out_loc.at[a]).start()
            else:
                remote(here, outs[a].at[:, cols(i)], out_send.at[a], out_recv.at[a], back(r))

    sums = (dk_s, dv_s)

    def rows_of(g, first_row, count):
        return pl.ds(g * B + first_row * G, count * G)

    def to_sib(g):
        for j in range(2):
            sib_buf[g, j] = sums[j][rows_of(g, 0, 2), :].astype(jnp.bfloat16)
        remote(sib_buf.at[g], sib_in.at[g], sib_send.at[g], sib_recv.at[g], sib)

    def to_z(g):
        wait_for(sib_in.at[g], sib_recv.at[g])
        for j in range(2):
            t = sums[j][rows_of(g, 2, 1), :] + sib_in[g, j, pl.ds(0, G)].astype(jnp.float32)
            z_buf[g, j] = t.astype(jnp.bfloat16)
        remote(z_buf.at[g], z_in.at[g], z_send.at[g], z_recv.at[g], zpart)

    def to_owner(g):
        wait_for(z_in.at[g], z_recv.at[g])
        for j in range(2):
            t = sums[j][rows_of(g, 3, 1), :] + sib_in[g, j, pl.ds(G, G)].astype(jnp.float32)
            fin[1 + j, pl.ds(g * G, G), :] = (t + z_in[g, j].astype(jnp.float32)).astype(jnp.bfloat16)
        send_back(1, g)
        send_back(2, g)

    def dq_send_parts(g):
        for s in (2, 1, 3):
            dqb[s - 1, g] = dqt[:, part(s, g)].T.astype(jnp.bfloat16)
            remote(
                dqb.at[s - 1, g], dq_in.at[s - 1, g], dq_send.at[s - 1, g], dq_recv.at[s - 1, g], ring(4 - s)
            )

    def dq_owner(g):
        dq = dqt[:, part(0, g)].T
        for s in (1, 3, 2):
            wait_for(dq_in.at[s - 1, g], dq_recv.at[s - 1, g])
            dq = dq + dq_in[s - 1, g].astype(jnp.float32)
        fin[0, pl.ds(g * G, G), :] = dq.astype(jnp.bfloat16)
        send_back(0, g)

    k1, k2, k3, k4 = (3, 1, 2, 0)
    soon = [g for g in (k1, k2, k3, k4) if g != d] + [d]
    for g in soon:
        stats_take(g)
        block(g, k1)
    to_sib(k1)
    block(k1, k2)
    block(k1, k3)
    to_z(k1)
    block(k1, k4)
    dq_send_parts(k1)
    block(k2, k2)
    block(k3, k2)
    block(k4, k2)
    to_sib(k2)
    block(k2, k3)
    block(k2, k4)
    to_z(k2)
    dq_send_parts(k2)
    to_owner(k1)
    block(k3, k3)
    block(k4, k3)
    to_sib(k3)
    dq_owner(k1)
    block(k3, k4)
    dq_send_parts(k3)
    block(k4, k4)
    to_sib(k4)
    dq_send_parts(k4)
    to_z(k3)
    to_z(k4)
    dq_owner(k2)
    to_owner(k2)
    dq_owner(k3)
    to_owner(k3)
    dq_owner(k4)
    to_owner(k4)

    for a in range(4):
        wait_for(qg.at[pl.ds(T, B - T), :], s1_send.at[a])
    wait_for(d_slot.at[pl.ds(1, H - 1)], d_send)
    for n in range(2):
        for s in range(3):
            for g in range(4):
                wait_for(kg.at[part(0, g), :], kv_send.at[n, s, g])
                wait_for(qg.at[part(0, g), :], qg_send.at[n, s, g])
    for g in range(4):
        for t in range(3):
            wait_for(st.at[g], st_send.at[t, g])
            wait_for(dqb.at[t, g], dq_send.at[t, g])
        wait_for(sib_buf.at[g], sib_send.at[g])
        wait_for(z_buf.at[g], z_send.at[g])
    for a in (1, 2, 0):
        wait_for(fin.at[a, pl.ds(T, B - T), :], out_send.at[a])
        wait_for(fin.at[a, pl.ds(0, T), :], out_loc.at[a])
        wait_for(fin.at[a, pl.ds(T, B - T), :], out_recv.at[a])


def attention_backward(nx, outer, inner, queries, keys, values, outputs, out_grads):
    T, W = queries.shape
    D = HEAD_DIM
    H = inner
    B = H * T
    NQ = 4 * B
    TK = min(256, B)
    bf, f32 = jnp.bfloat16, jnp.float32
    dma = pltpu.SemaphoreType.DMA
    vm = pltpu.VMEM
    hbm = pl.BlockSpec(memory_space=pltpu.HBM)
    return pl.pallas_call(
        functools.partial(kernel, (H, nx, outer // 4, T, TK)),
        out_shape=[jax.ShapeDtypeStruct((T, W), bf)] * 3,
        in_specs=[hbm] * 5,
        out_specs=[hbm] * 3,
        scratch_shapes=[
            vm((NQ, D), bf), vm((NQ, D), bf), vm((NQ, D), bf), vm((NQ, D), bf),
            vm((D, NQ), bf),
            vm((NQ, NQ), f32),
            vm((NQ // TK, NQ), f32), vm((NQ // TK, NQ), f32), vm((NQ // TK, NQ), f32),
            vm((T, W), bf), vm((T, W), bf),
            vm((H, 1, 128), f32), vm((H, 1, 128), f32),
            vm((8, NQ), f32),
            vm((4, 1, B + 128), f32), vm((3, 4, 1, B + 128), f32),
            vm((D, NQ), f32),
            vm((NQ, D), f32), vm((NQ, D), f32),
            vm((4, 2, B // 2, D), bf), vm((4, 2, B // 2, D), bf),
            vm((4, 2, B // 4, D), bf), vm((4, 2, B // 4, D), bf),
            vm((3, 4, B // 4, D), bf), vm((3, 4, B // 4, D), bf),
            vm((3, B, D), bf),
            dma((2,)), dma((4,)), dma((4, 4)), dma((4,)), dma, dma,
            dma((2, 3, 4)), dma((2, 3, 4)), dma((2, 3, 4)), dma((2, 3, 4)), dma((3, 4)), dma((3, 4)),
            dma((4,)), dma((4,)), dma((4,)), dma((4,)), dma((3, 4)), dma((3, 4)), dma((3,)), dma((3,)), dma((3,)),
        ],
        compiler_params=pltpu.CompilerParams(
            collective_id=0, has_side_effects=True, vmem_limit_bytes=VMEM_LIMIT
        ),
        cost_estimate=pl.CostEstimate(flops=6 * 10**9, bytes_accessed=10**6, transcendentals=4 * 10**6),
    )(queries, keys, values, outputs, out_grads)


def solution(mesh, nx=4):
    spec = P(("outer", "inner"), None)
    return jax.shard_map(
        functools.partial(attention_backward, nx, mesh.shape["outer"], mesh.shape["inner"]),
        mesh=mesh,
        in_specs=(spec,) * 5,
        out_specs=(spec,) * 3,
        check_vma=False,
    )
```

time: 383 us -> 62 us (0.16)
  waiting for transfers between devices: 170 us -> 0 us
  matrix products: 109 us -> 0 us
  Pallas kernels: 0 us -> 57.7 us
  starting transfers between devices: 42.2 us -> 0 us
  blocking collectives: 20.7 us -> 0 us
  between operations: 14 us -> 0.65 us
  other arithmetic: 9.47 us -> 0 us
  local copies, waits for them, and re-layouts: 12.1 us -> 3.21 us
    reduce_scatter x2 -> x0, waiting for transfers between devices: 114 us -> none  [the longest x1 58.5 us: body(): lax.psum_scatter(value_parts.reshape(all_rows, head_loc, HEAD_DIM), 'oute...]
    dot_general x96 -> x0, matrix products: 109 us -> none  [the longest x32 38.9 us: score_block(): jnp.einsum('qhd,khd->hqk', query_rows, key_rows, preferred_element_type=j...]
    pallas_call x0 -> x1, Pallas kernels: none -> 57.7 us  [attention_backward(): pl.pallas_call(functools.partial(kernel, (H, nx, outer // 4, T, TK)), out...]
    all_to_all x7 -> x0, starting transfers between devices: 42 us -> none  [the longest x1 10 us: body(): lax.all_to_all(key_acc.astype(jnp.bfloat16), 'inner', split_axis=0, conca...]
    all_to_all x7 -> x0, waiting for transfers between devices: 39.5 us -> none  [the longest x1 8.38 us: body(): lax.all_to_all(split_heads(queries), 'inner', split_axis=1, concat_axis=0...]
    all_to_all x1 -> x0, blocking collectives: 20.7 us -> none  [body(): lax.all_to_all(split_heads(keys), 'inner', split_axis=1, concat_axis=0, t...]
    all_gather x2 -> x0, waiting for transfers between devices: 15.3 us -> none  [the longest x1 15.3 us: body(): lax.all_gather(values_here, 'outer', axis=0, tiled=True)]
    reshape x6 -> x0, local copies, waits for them, and re-layouts: 7.11 us -> none  [the longest x5 6.36 us: split_heads(): return array.reshape(tok_rows, heads_all, HEAD_DIM)]
  transfers between devices with their start and end apart: 11 -> 0, of which waited for: 8 -> 0; matrix products, arithmetic and copies ran while one was open for 10% -> 0% of each run, Pallas kernels for 0% -> 0%
where the time goes in v1:
time: 62 us; the launch traced here: 61.6 us
  Pallas kernels  57.7 us (93%)
  local copies, waits for them, and re-layouts  3.21 us (5%)
  between operations  0.65 us (1%)
    pallas_call x1, Pallas kernels, attention_backward(): pl.pallas_call(functools.partial(kernel, (H, nx, outer // 4, T, TK)), out...  57.7 us
    unnamed x7, local copies, waits for them, and re-layouts  3.21 us

profile of v1, /device:TPU:1, one launch (start us, length us, event | category | flops | bytes accessed | tf_op | source)
XLA Modules:
  0.0 61.6 jit_solution(24343582875417483)
XLA Ops:
  0.6 57.7 %shard_map.76 = (bf16[32,2048]{1,0:T(8,128)(2,1)}, bf16[32,2048]{1,0:T(8,128)(2,1)}, bf16[32,2048]{1,0:T(8,128)(2,1)}) custom-call(bf16[32,2048]{1,0:T(8,128)(2,1)} %q_in.1, bf16[32,2048]{1,0:T(8,128)(2,1)} %k_in.1, bf16[32,2048]{1,0:T(8,128)(2,1)} %v_in.1, bf16[32,2048]{1,0:T(8,128)(2,1)} %o_in.1, bf16[32,2048]{1,0:T(8,128)(2,1)} %g_in.1), custom_call_target="tpu_custom_call" | custom-call | flops 6000000000 | bytes 1000000 | tf_op jit(solution)/shard_map/pallas_call | solution.py:396
  58.3 0.0 copy-start.1
  58.3 1.6 %copy.11 = bf16[32,2048]{1,0:T(8,128)(2,1)} copy(bf16[32,2048]{1,0:T(8,128)(2,1)} %get-tuple-element.6) | data formatting | bytes 262144
  60.0 0.0 copy-done.1
  60.0 0.0 copy-start
  60.0 0.7 %copy.12 = bf16[32,2048]{1,0:T(8,128)(2,1)} copy(bf16[32,2048]{1,0:T(8,128)(2,1)S(1)} %copy-done.1) | data formatting | bytes 262144
  60.6 0.3 copy-done
  60.9 0.7 %copy.13 = bf16[32,2048]{1,0:T(8,128)(2,1)} copy(bf16[32,2048]{1,0:T(8,128)(2,1)S(1)} %copy-done) | data formatting | bytes 262144
Async XLA Ops:
  58.3 1.6 %copy-start.1 = (bf16[32,2048]{1,0:T(8,128)(2,1)S(1)}, bf16[32,2048]{1,0:T(8,128)(2,1)}, u32[]{:S(2)}) copy-start(bf16[32,2048]{1,0:T(8,128)(2,1)} %get-tuple-element.7) | copy-start | bytes 393220
  60.0 1.0 %copy-start = (bf16[32,2048]{1,0:T(8,128)(2,1)S(1)}, bf16[32,2048]{1,0:T(8,128)(2,1)}, u32[]{:S(2)}) copy-start(bf16[32,2048]{1,0:T(8,128)(2,1)} %get-tuple-element.8) | copy-start | bytes 393220

commit v2 on v1

--- a/solution.py
+++ b/solution.py
@@ -127,8 +127,6 @@
                     )
 
     s1_sends((0, 1))
-    if VG_AT == 0:
-        s1_sends((2, 3))
 
     cp_g.wait()
     cp_o.wait()
@@ -229,20 +227,20 @@
     forward(0, d)
     complete(0, b)
     stats((a, b), (b, a), (b, b))
+    first(1, a)
     complete(0, c3)
     stats((a, c3), (b, c3), (c3, a), (c3, b), (c3, c3))
-    first(1, a)
+    first(1, b)
     complete(0, d)
+    stats((a, d), (b, d), (c3, d))
+    first(1, c3)
     wait_for(d_slot.at[pl.ds(1, H - 1)], d_recv)
-    stats((a, d), (b, d), (c3, d))
     for g in (a, b, c3):
         stats_send(g)
-    first(1, b)
+    forward(1, a)
+    first(1, d)
     stats((d, a), (d, b), (d, c3), (d, d))
     stats_send(d)
-    first(1, c3)
-    forward(1, a)
-    first(1, d)
     for g in (b, c3, d):
         forward(1, g)
     for g in range(4):
@@ -349,13 +347,13 @@
     to_sib(k3)
     dq_owner(k1)
     block(k3, k4)
+    to_z(k3)
     dq_send_parts(k3)
     block(k4, k4)
     to_sib(k4)
     dq_send_parts(k4)
-    to_z(k3)
+    dq_owner(k2)
     to_z(k4)
-    dq_owner(k2)
     to_owner(k2)
     dq_owner(k3)
     to_owner(k3)
@@ -382,6 +380,12 @@
         wait_for(fin.at[a, pl.ds(T, B - T), :], out_recv.at[a])
 
 
+def hand_over(a_in, b_in, c_in, a_out, b_out, c_out):
+    a_out[...] = a_in[...]
+    b_out[...] = b_in[...]
+    c_out[...] = c_in[...]
+
+
 def attention_backward(nx, outer, inner, queries, keys, values, outputs, out_grads):
     T, W = queries.shape
     D = HEAD_DIM
@@ -393,7 +397,7 @@
     dma = pltpu.SemaphoreType.DMA
     vm = pltpu.VMEM
     hbm = pl.BlockSpec(memory_space=pltpu.HBM)
-    return pl.pallas_call(
+    grads = pl.pallas_call(
         functools.partial(kernel, (H, nx, outer // 4, T, TK)),
         out_shape=[jax.ShapeDtypeStruct((T, W), bf)] * 3,
         in_specs=[hbm] * 5,
@@ -422,6 +426,13 @@
         ),
         cost_estimate=pl.CostEstimate(flops=6 * 10**9, bytes_accessed=10**6, transcendentals=4 * 10**6),
     )(queries, keys, values, outputs, out_grads)
+    vmem = pl.BlockSpec(memory_space=pltpu.VMEM)
+    return pl.pallas_call(
+        hand_over,
+        out_shape=[jax.ShapeDtypeStruct((T, W), bf)] * 3,
+        in_specs=[vmem] * 3,
+        out_specs=[vmem] * 3,
+    )(*grads)
 
 
 def solution(mesh, nx=4):

time: 62 us -> 58.7 us (0.947)
  local copies, waits for them, and re-layouts: 3.21 us -> 0 us
    unnamed x7 -> x0, local copies, waits for them, and re-layouts: 3.21 us -> none
    pallas_call x0 -> x1, Pallas kernels: none -> 1.78 us  [attention_backward(): pl.pallas_call(hand_over, out_shape=[jax.ShapeDtypeStruct((T, W), bf)] *...]
    pallas_call x1, Pallas kernels: 57.7 us -> 56.2 us  [attention_backward(): pl.pallas_call(functools.partial(kernel, (H, nx, outer // 4, T, TK)), out...]
where the time goes in v2:
time: 58.7 us; the launch traced here: 58.6 us
  Pallas kernels  58 us (99%)
  between operations  0.64 us (1%)
    pallas_call x1, Pallas kernels, attention_backward(): pl.pallas_call(functools.partial(kernel, (H, nx, outer // 4, T, TK)), out...  56.2 us
    pallas_call x1, Pallas kernels, attention_backward(): pl.pallas_call(hand_over, out_shape=[jax.ShapeDtypeStruct((T, W), bf)] *...  1.78 us

profile of v2, /device:TPU:1, one launch (start us, length us, event | category | flops | bytes accessed | tf_op | source)
XLA Modules:
  0.0 58.6 jit_solution(18382986346234545587)
XLA Ops:
  0.6 56.2 %shard_map.76 = (bf16[32,2048]{1,0:T(8,128)(2,1)}, bf16[32,2048]{1,0:T(8,128)(2,1)}, bf16[32,2048]{1,0:T(8,128)(2,1)}) custom-call(bf16[32,2048]{1,0:T(8,128)(2,1)} %q_in.1, bf16[32,2048]{1,0:T(8,128)(2,1)} %k_in.1, bf16[32,2048]{1,0:T(8,128)(2,1)} %v_in.1, bf16[32,2048]{1,0:T(8,128)(2,1)} %o_in.1, bf16[32,2048]{1,0:T(8,128)(2,1)} %g_in.1), custom_call_target="tpu_custom_call" | custom-call | flops 6000000000 | bytes 1000000 | tf_op jit(solution)/shard_map/pallas_call | solution.py:400
  56.8 1.8 %shard_map.77 = (bf16[32,2048]{1,0:T(8,128)(2,1)}, bf16[32,2048]{1,0:T(8,128)(2,1)}, bf16[32,2048]{1,0:T(8,128)(2,1)}) custom-call(bf16[32,2048]{1,0:T(8,128)(2,1)} %get-tuple-element.6.a_in, bf16[32,2048]{1,0:T(8,128)(2,1)} %get-tuple-element.7.b_in, bf16[32,2048]{1,0:T(8,128)(2,1)} %get-tuple-element.8.c_in), custom_call_target="tpu_custom_call" | custom-call | tf_op jit(solution)/shard_map/pallas_call | solution.py:430

commit v3 on v2

--- a/solution.py
+++ b/solution.py
@@ -16,6 +16,7 @@
 S1_ORDER = (0, 2, 1, 3)
 VMEM_LIMIT = 62 << 20
 VG_AT = 3
+AHEAD = 2
 
 
 def dot(a, b, dims):
@@ -25,9 +26,9 @@
 def kernel(
     cfg,
     q_in, k_in, v_in, o_in, g_in,
-    dq_out, dk_out, dv_out,
+    out,
     qg, kg, vg, gg, kt, e_s, m_s, l_s, f_s,
-    own_o, own_g, d_stage, d_slot, d_all, st, st_in, dqt, dk_s, dv_s, sib_buf, sib_in, z_buf, z_in, dqb, dq_in, fin,
+    own_o, own_g, d_stage, d_slot, d_all, st, st_in, dqt, dk_s, dv_s, dp_s, sib_buf, sib_in, z_buf, z_in, dqb, dq_in, fin,
     in_sem, s1_send, s1_recv, s1_loc, d_send, d_recv,
     kv_send, kv_recv, qg_send, qg_recv, st_send, st_recv,
     sib_send, sib_recv, z_send, z_recv, dq_send, dq_recv, out_send, out_recv, out_loc,
@@ -67,7 +68,6 @@
 
     sib = dev(z, y, 1 - c, x)
     zpart = dev(z - up, y, c, x)
-    diag = dev(z - up, y, 1 - c, x)
 
     def ring(t):
         return dev(z, lax.rem(y + t, NY), c, x)
@@ -90,7 +90,7 @@
 
     barrier = pltpu.get_barrier_semaphore()
     partners = [there(r) for r in range(H - 1, 0, -1)] + [back(NX + dx) for dx in range(NX)]
-    partners += [ring(2), ring(1), ring(3), diag, zpart, sib]
+    partners += [ring(2), ring(1), ring(3), zpart, sib]
     for p in partners:
         pl.semaphore_signal(barrier, inc=1, device_id=p, device_id_type=MESH)
 
@@ -245,8 +245,15 @@
         forward(1, g)
     for g in range(4):
         transpose_keys(g)
-    for g in range(4):
-        complete(1, g)
+    ahead = {}
+    for n in range(AHEAD):
+        complete(1, S1_ORDER[n])
+        new = [(S1_ORDER[n], S1_ORDER[j]) for j in range(n + 1)] + [(S1_ORDER[j], S1_ORDER[n]) for j in range(n)]
+        for gq, gk in new:
+            ahead[gq, gk] = len(ahead)
+            dp_s[ahead[gq, gk]] = dot(vg[group(gk), :], gg[group(gq), :], NT)
+    for n in range(AHEAD, 4):
+        complete(1, S1_ORDER[n])
 
     seen = set()
 
@@ -255,7 +262,7 @@
         seen.update(((gq, "q"), (gk, "k")))
         gv = gg[group(gq), :]
         qv = qg[group(gq), :]
-        dp = dot(vg[group(gk), :], gv, NT)
+        dp = dp_s[ahead[gq, gk]] if (gq, gk) in ahead else dot(vg[group(gk), :], gv, NT)
         p = jnp.concatenate(
             [
                 e_s[pl.ds(gk * B + h * TK, TK), group(gq)] * f_s[pl.ds(gk * halves + h, 1), group(gq)]
@@ -271,16 +278,15 @@
         dk_s[group(gk), :] = dk if start_k else dk_s[group(gk), :] + dk
         dqt[:, group(gq)] = dq if start_q else dqt[:, group(gq)] + dq
 
-    outs = (dq_out, dk_out, dv_out)
-
-    def send_back(a, g):
+    def send_back(n, g):
+        pick = pl.ds(n, n + 1)
         for j in range(per):
             r = g * per + j
-            here = fin.at[a, pl.ds(r * T, T), :]
+            here = fin.at[pick, pl.ds(r * T, T), :]
             if r == 0:
-                pltpu.make_async_copy(here, outs[a].at[:, cols(i)], out_loc.at[a]).start()
+                pltpu.make_async_copy(here, out.at[pick, :, cols(i)], out_loc.at[n]).start()
             else:
-                remote(here, outs[a].at[:, cols(i)], out_send.at[a], out_recv.at[a], back(r))
+                remote(here, out.at[pick, :, cols(i)], out_send.at[n], out_recv.at[n], back(r))
 
     sums = (dk_s, dv_s)
 
@@ -305,11 +311,10 @@
             t = sums[j][rows_of(g, 3, 1), :] + sib_in[g, j, pl.ds(G, G)].astype(jnp.float32)
             fin[1 + j, pl.ds(g * G, G), :] = (t + z_in[g, j].astype(jnp.float32)).astype(jnp.bfloat16)
         send_back(1, g)
-        send_back(2, g)
 
     def dq_send_parts(g):
         for s in (2, 1, 3):
-            dqb[s - 1, g] = dqt[:, part(s, g)].T.astype(jnp.bfloat16)
+            dqb[s - 1, g] = dqt[:, part(s, g)].astype(jnp.bfloat16).T
             remote(
                 dqb.at[s - 1, g], dq_in.at[s - 1, g], dq_send.at[s - 1, g], dq_recv.at[s - 1, g], ring(4 - s)
             )
@@ -347,8 +352,8 @@
     to_sib(k3)
     dq_owner(k1)
     block(k3, k4)
+    dq_send_parts(k3)
     to_z(k3)
-    dq_send_parts(k3)
     block(k4, k4)
     to_sib(k4)
     dq_send_parts(k4)
@@ -374,16 +379,17 @@
             wait_for(dqb.at[t, g], dq_send.at[t, g])
         wait_for(sib_buf.at[g], sib_send.at[g])
         wait_for(z_buf.at[g], z_send.at[g])
-    for a in (1, 2, 0):
-        wait_for(fin.at[a, pl.ds(T, B - T), :], out_send.at[a])
-        wait_for(fin.at[a, pl.ds(0, T), :], out_loc.at[a])
-        wait_for(fin.at[a, pl.ds(T, B - T), :], out_recv.at[a])
-
-
-def hand_over(a_in, b_in, c_in, a_out, b_out, c_out):
-    a_out[...] = a_in[...]
-    b_out[...] = b_in[...]
-    c_out[...] = c_in[...]
+    for n in (1, 0):
+        pick = pl.ds(n, n + 1)
+        wait_for(fin.at[pick, pl.ds(T, B - T), :], out_send.at[n])
+        wait_for(fin.at[pick, pl.ds(0, T), :], out_loc.at[n])
+        wait_for(fin.at[pick, pl.ds(T, B - T), :], out_recv.at[n])
+
+
+def hand_over(grads, dq_out, dk_out, dv_out):
+    dq_out[...] = grads[0]
+    dk_out[...] = grads[1]
+    dv_out[...] = grads[2]
 
 
 def attention_backward(nx, outer, inner, queries, keys, values, outputs, out_grads):
@@ -399,9 +405,9 @@
     hbm = pl.BlockSpec(memory_space=pltpu.HBM)
     grads = pl.pallas_call(
         functools.partial(kernel, (H, nx, outer // 4, T, TK)),
-        out_shape=[jax.ShapeDtypeStruct((T, W), bf)] * 3,
+        out_shape=jax.ShapeDtypeStruct((3, T, W), bf),
         in_specs=[hbm] * 5,
-        out_specs=[hbm] * 3,
+        out_specs=hbm,
         scratch_shapes=[
             vm((NQ, D), bf), vm((NQ, D), bf), vm((NQ, D), bf), vm((NQ, D), bf),
             vm((D, NQ), bf),
@@ -413,13 +419,14 @@
             vm((4, 1, B + 128), f32), vm((3, 4, 1, B + 128), f32),
             vm((D, NQ), f32),
             vm((NQ, D), f32), vm((NQ, D), f32),
+            vm((max(AHEAD * AHEAD, 1), B, B), f32),
             vm((4, 2, B // 2, D), bf), vm((4, 2, B // 2, D), bf),
             vm((4, 2, B // 4, D), bf), vm((4, 2, B // 4, D), bf),
             vm((3, 4, B // 4, D), bf), vm((3, 4, B // 4, D), bf),
             vm((3, B, D), bf),
             dma((2,)), dma((4,)), dma((4, 4)), dma((4,)), dma, dma,
             dma((2, 3, 4)), dma((2, 3, 4)), dma((2, 3, 4)), dma((2, 3, 4)), dma((3, 4)), dma((3, 4)),
-            dma((4,)), dma((4,)), dma((4,)), dma((4,)), dma((3, 4)), dma((3, 4)), dma((3,)), dma((3,)), dma((3,)),
+            dma((4,)), dma((4,)), dma((4,)), dma((4,)), dma((3, 4)), dma((3, 4)), dma((2,)), dma((2,)), dma((2,)),
         ],
         compiler_params=pltpu.CompilerParams(
             collective_id=0, has_side_effects=True, vmem_limit_bytes=VMEM_LIMIT
@@ -430,9 +437,9 @@
     return pl.pallas_call(
         hand_over,
         out_shape=[jax.ShapeDtypeStruct((T, W), bf)] * 3,
-        in_specs=[vmem] * 3,
+        in_specs=[vmem],
         out_specs=[vmem] * 3,
-    )(*grads)
+    )(grads)
 
 
 def solution(mesh, nx=4):

time: 58.7 us -> 58.5 us (level)
  no operation moved by 1% of the time
where the time goes in v3:
time: 58.5 us; the launch traced here: 58.4 us
  Pallas kernels  57.8 us (99%)
  between operations  0.64 us (1%)
    pallas_call x1, Pallas kernels, attention_backward(): pl.pallas_call(functools.partial(kernel, (H, nx, outer // 4, T, TK)), out...  56 us
    pallas_call x1, Pallas kernels, attention_backward(): pl.pallas_call(hand_over, out_shape=[jax.ShapeDtypeStruct((T, W), bf)] *...  1.75 us

profile of v3, /device:TPU:1, one launch (start us, length us, event | category | flops | bytes accessed | tf_op | source)
XLA Modules:
  0.0 58.4 jit_solution(358504048847705234)
XLA Ops:
  0.6 56.0 %shard_map.76.grads = bf16[3,32,2048]{2,1,0:T(8,128)(2,1)} custom-call(bf16[32,2048]{1,0:T(8,128)(2,1)} %q_in.1, bf16[32,2048]{1,0:T(8,128)(2,1)} %k_in.1, bf16[32,2048]{1,0:T(8,128)(2,1)} %v_in.1, bf16[32,2048]{1,0:T(8,128)(2,1)} %o_in.1, bf16[32,2048]{1,0:T(8,128)(2,1)} %g_in.1), custom_call_target="tpu_custom_call" | custom-call | flops 6000000000 | bytes 1000000 | tf_op jit(solution)/shard_map/pallas_call | solution.py:406
  56.7 1.7 %shard_map.77 = (bf16[32,2048]{1,0:T(8,128)(2,1)}, bf16[32,2048]{1,0:T(8,128)(2,1)}, bf16[32,2048]{1,0:T(8,128)(2,1)}) custom-call(bf16[3,32,2048]{2,1,0:T(8,128)(2,1)} %shard_map.76.grads), custom_call_target="tpu_custom_call" | custom-call | tf_op jit(solution)/shard_map/pallas_call | solution.py:437

commit v4 on v3

--- a/solution.py
+++ b/solution.py
@@ -357,8 +357,8 @@
     block(k4, k4)
     to_sib(k4)
     dq_send_parts(k4)
+    to_z(k4)
     dq_owner(k2)
-    to_z(k4)
     to_owner(k2)
     dq_owner(k3)
     to_owner(k3)

time: 58.5 us -> 58.6 us (level)
  no operation moved by 1% of the time
where the time goes in v4:
time: 58.6 us; the launch traced here: 58.5 us
  Pallas kernels  57.8 us (99%)
  between operations  0.64 us (1%)
    pallas_call x1, Pallas kernels, attention_backward(): pl.pallas_call(functools.partial(kernel, (H, nx, outer // 4, T, TK)), out...  56.1 us
    pallas_call x1, Pallas kernels, attention_backward(): pl.pallas_call(hand_over, out_shape=[jax.ShapeDtypeStruct((T, W), bf)] *...  1.75 us

profile of v4, /device:TPU:1, one launch (start us, length us, event | category | flops | bytes accessed | tf_op | source)
XLA Modules:
  0.0 58.5 jit_solution(15746527385927913686)
XLA Ops:
  0.6 56.1 %shard_map.76.grads = bf16[3,32,2048]{2,1,0:T(8,128)(2,1)} custom-call(bf16[32,2048]{1,0:T(8,128)(2,1)} %q_in.1, bf16[32,2048]{1,0:T(8,128)(2,1)} %k_in.1, bf16[32,2048]{1,0:T(8,128)(2,1)} %v_in.1, bf16[32,2048]{1,0:T(8,128)(2,1)} %o_in.1, bf16[32,2048]{1,0:T(8,128)(2,1)} %g_in.1), custom_call_target="tpu_custom_call" | custom-call | flops 6000000000 | bytes 1000000 | tf_op jit(solution)/shard_map/pallas_call | solution.py:406
  56.7 1.7 %shard_map.77 = (bf16[32,2048]{1,0:T(8,128)(2,1)}, bf16[32,2048]{1,0:T(8,128)(2,1)}, bf16[32,2048]{1,0:T(8,128)(2,1)}) custom-call(bf16[3,32,2048]{2,1,0:T(8,128)(2,1)} %shard_map.76.grads), custom_call_target="tpu_custom_call" | custom-call | tf_op jit(solution)/shard_map/pallas_call | solution.py:437
